TPU v7x, 256 devices: a whole 4x4x8 slice. The times are simulated.
256 devices in a mesh: gx: 32 (over z, y), gy: 2 (over core), gz: 4 (over x).
Axes of the slice: x: 4, y: 4, z: 8, core: 2. Of those that a mesh axis runs over, the one named last changes fastest.
Arguments:
- snapshot: float32 [1024, 512, 512], P('gx', 'gy', 'gz'), may hold values from -6 to 6
- factor_x: float32 [1024, 128], P('gx'), may hold values from -0.375 to 0.375
- factor_y: float32 [512, 128], P('gy'), may hold values from -0.375 to 0.375
- factor_z: float32 [512, 128], P('gz'), may hold values from -0.375 to 0.375
Outputs:
- core: float32 [128, 128, 128], P('gx', 'gy', 'gz')
All inputs are finite; a program needn't handle non-finite values.
Results may differ from a plain program's by a relative error of at most 0.00007.
Values sent between devices are 32-bit elements; how exact they have to be, the bound alone decides.
A program may use at most 64 MiB of HBM per device.

v0:
```python
import functools

import jax
import jax.numpy as jnp
from jax import lax
from jax.experimental import pallas as pl
from jax.experimental.pallas import tpu as pltpu
from jax.sharding import PartitionSpec as P

MESH = pl.DeviceIdType.MESH
F32, BF16 = jnp.float32, jnp.bfloat16
NT = (((1,), (1,)), ((), ()))
CHUNKS = 2
WIDTH = 8 // CHUNKS
PAIRS = WIDTH // 2


def split(value):
    high = value.astype(BF16)
    return high, (value - high.astype(F32)).astype(BF16)


def rows(start, size):
    return pl.ds(pl.multiple_of(start, 8), size)


def stacked(factor_t):
    high, low = split(factor_t)
    top = jnp.concatenate([high, high], axis=1)
    return jnp.concatenate([top, jnp.concatenate([low, jnp.zeros_like(low)], axis=1)], axis=0)


def kernel(
    zn, snap, fx, fy, fz, out,
    s_buf, fy_v, fz_v, fxg, ft, fyl, fzl, fxl, t1s, t1o, t1r, t3, rx, rx1, p, zr, fin,
    s_sem, f_sem, ys, yr, r_s, r_r, x_s, x_r, z_s, z_r, g_s, g_r,
):
    gx, core, xi = lax.axis_index("gx"), lax.axis_index("gy"), lax.axis_index("gz")
    zi, yi = gx // 4, lax.rem(gx, 4)
    other = 1 - core
    plane = xi * 4 + yi
    planes = 4 * zn

    right, opposite, left = lax.rem(xi + 1, 4), lax.rem(xi + 2, 4), lax.rem(xi + 3, 4)

    def in_plane(d):
        x, y = lax.rem(xi + d // 4, 4), lax.rem(yi + lax.rem(d, 4), 4)
        return (zi * 4 + y, core, x)

    def in_column(d):
        z, y = lax.rem(zi + d // 4, zn), lax.rem(yi + lax.rem(d, 4), 4)
        return z * 4 + y, (z * 4 + y, core, xi)

    def load(i):
        return pltpu.make_async_copy(snap.at[:, i], s_buf.at[i], s_sem.at[i])

    load_y = pltpu.make_async_copy(fy, fy_v, f_sem.at[0])
    load_z = pltpu.make_async_copy(fz, fz_v, f_sem.at[1])
    my_fx = fxg.at[rows(yi * 32, 32)]
    load_x = pltpu.make_async_copy(fx, my_fx, f_sem.at[2])
    load_y.start()

    @pl.loop(0, 16)
    def _(i):
        load(i).start()

    load_z.start()
    load_x.start()

    barrier = pltpu.get_barrier_semaphore()
    pl.semaphore_signal(barrier, inc=1, device_id=(gx, other, xi), device_id_type=MESH)

    @pl.loop(1, 16)
    def _(d):
        pl.semaphore_signal(barrier, inc=1, device_id=in_plane(d), device_id_type=MESH)

    @pl.loop(1, zn)
    def _(d):
        pl.semaphore_signal(barrier, inc=1, device_id=in_column(4 * d)[1], device_id_type=MESH)

    load_y.wait()
    ft[...] = fy_v[...].T
    high, low = split(jnp.concatenate([ft[rows(other * 64, 64)], ft[rows(core * 64, 64)]], axis=0))
    fyl[...] = jnp.concatenate([high, low], axis=0)
    load_z.wait()
    group = 4 * WIDTH
    fz_t = fz_v[...].T
    fzl[...] = stacked(jnp.concatenate(
        [fz_t[32 * x + group * j:32 * x + group * (j + 1)] for j in range(CHUNKS) for x in range(4)], axis=0))

    def first_of(i):
        load(i).wait()
        high, low = split(jnp.concatenate([s_buf[i, 0], s_buf[i, 1]], axis=1))
        both = jnp.dot(fyl[...], high, preferred_element_type=F32)
        t = both[:128] + both[128:] + jnp.dot(fyl[0:128], low, preferred_element_type=F32)
        t1s[i, 0:64] = t[:64, :128]
        t1s[i, 64:128] = t[:64, 128:]
        t1o[i, 0:64] = t[64:, :128]
        t1o[i, 64:128] = t[64:, 128:]

    def swap(part):
        at = pl.ds(4 * part, 4)
        return pltpu.make_async_remote_copy(
            src_ref=t1s.at[at], dst_ref=t1r.at[at], send_sem=ys.at[part], recv_sem=yr.at[part],
            device_id=(gx, other, xi), device_id_type=MESH)

    def second_of(part):
        swap(part).wait_recv()
        for i in range(2):
            n = 4 * part + 2 * i
            t2 = (t1o[n:n + 2] + t1r[n:n + 2]).reshape(256, 128)
            w = jnp.concatenate(split(t2), axis=1)
            q = lax.dot_general(fzl[...], w, NT, preferred_element_type=F32)
            q = q[:128] + q[128:]
            t3[pl.ds(n, 128, stride=16), :] = q[:, :128]
            t3[pl.ds(n + 1, 128, stride=16), :] = q[:, 128:]

    def block_of(part, x, y, number):
        j, h = part[:2]
        at = ((j * 4 + x) * 4 + y) * WIDTH
        if h is None:
            return t3.at[pl.ds(pl.multiple_of(at * 16, 32), number * 16)]
        return t3.reshape(128, 2, 8, 128).at[pl.ds(at, number), h]

    def slot_of(ref, part, at):
        j, h = part[:2]
        if h is None:
            return ref.at[j, at]
        return ref.reshape(*ref.shape[:-2], ref.shape[-2] // 16, 2, 8, 128).at[j, at, :, h]

    def relay(part, way):
        return pltpu.make_async_remote_copy(
            src_ref=block_of(part, opposite, 2 * way, 2 * WIDTH), dst_ref=slot_of(rx1, part, way),
            send_sem=r_s.at[part[2], way], recv_sem=r_r.at[part[2], way],
            device_id=(gx, core, (right, left)[way]), device_id_type=MESH)

    def send_relay(part):
        for way in range(2):
            relay(part, way).start()

    def exchange(part, x, y, slot):
        pltpu.make_async_remote_copy(
            src_ref=block_of(part, x, y, WIDTH), dst_ref=slot_of(rx, part, slot * 4 + yi),
            send_sem=x_s.at[part[2]], recv_sem=x_r.at[part[2]],
            device_id=(zi * 4 + y, core, x), device_id_type=MESH).start()

    def send_plain(part):
        @pl.loop(1, 4)
        def _(d):
            exchange(part, xi, lax.rem(yi + d, 4), 1)

        @pl.loop(0, 2)
        def _(y):
            exchange(part, right, y + 2, 0)
            exchange(part, left, y, 2)

    def send_merged(part):
        for way in range(2):
            relay(part, way).wait_recv()
            to = block_of(part, (right, left)[way], 2 * way, 2 * WIDTH)
            to[...] = to[...] + slot_of(rx1, part, way)[...]

        @pl.loop(0, 2)
        def _(y):
            exchange(part, right, y, 0)
            exchange(part, left, y + 2, 2)

    def spread(j, d):
        block, to = in_column(d)
        return pltpu.make_async_remote_copy(
            src_ref=p.at[j, block], dst_ref=zr.at[j, gx],
            send_sem=z_s.at[j], recv_sem=z_r.at[j], device_id=to, device_id_type=MESH)

    def gather_fx(d):
        y = lax.rem(yi + d, 4)
        return pltpu.make_async_remote_copy(
            src_ref=my_fx, dst_ref=my_fx, send_sem=g_s, recv_sem=g_r,
            device_id=(zi * 4 + y, core, xi), device_id_type=MESH)

    dummy = t3

    def wait(ref, sem):
        pltpu.make_async_copy(ref, ref, sem).wait()

    parts = [(0, 0, 0), (0, 1, 1)] + [(j, None, 1 + j) for j in range(1, CHUNKS)]

    def contract(j):
        add = rx[j, 0:4] + rx[j, 4:8] + rx[j, 8:12]
        turned = pltpu.roll(add.reshape(-1, 128), 64, 1).reshape(add.shape)
        low_half = lax.broadcasted_iota(jnp.int32, (16, 128), 1) < 64
        columns = []
        for q in range(PAIRS):
            c0, c1 = slice(16 * q, 16 * q + 16), slice(16 * (PAIRS + q), 16 * (PAIRS + q) + 16)
            pieces = []
            for y in range(4):
                pieces.append(jnp.where(low_half, add[y, c0], turned[y, c1]))
                pieces.append(jnp.where(low_half, turned[y, c0], add[y, c1]))
            columns.append(jnp.concatenate(pieces, axis=0))
        w = jnp.concatenate(split(jnp.concatenate(columns, axis=1)), axis=0)
        r = jnp.dot(fxl[...], w, preferred_element_type=F32)
        r = r[:128] + r[128:]
        for q in range(PAIRS):
            p[j, :, 4 * q:4 * q + 4] = r[:, 128 * q:128 * q + 128].reshape(planes, 4, 128)

    def total(j):
        w = zr[j, 0:4]
        for z in range(1, zn):
            w = w + zr[j, 4 * z:4 * z + 4]
        for y in range(4):
            turned = pltpu.roll(w[y], 64, 1)
            at = (j * 4 + y) * WIDTH * 4
            fin[at:at + 4 * PAIRS] = w[y]
            fin[at + 4 * PAIRS:at + 8 * PAIRS] = turned

    def do_spread(j):
        contract(j)

        @pl.loop(0, planes - 1)
        def _(i):
            k = i // 4
            z = lax.rem(zn // 2 + (k + 1) // 2 * (1 - 2 * lax.rem(k, 2)) + zn, zn)
            spread(j, 4 * z + 3 - lax.rem(i, 4)).start()

        zr[j, gx] = p[j, gx]

    def await_part(n):
        size = slice(0, 11 * WIDTH * 16 // (2 if n < 2 else 1))
        wait(dummy.at[size], x_r.at[n])

    def first(part):
        @pl.loop(4 * part, 4 * part + 4)
        def _(i):
            first_of(i)

    entered = lambda: pl.semaphore_wait(barrier, 1 + 15 + (zn - 1))
    for part in range(4):
        first(part)
        if part == 1:
            load_x.wait()
            entered()
            for n in range(part):
                swap(n).start()
        if part >= 1:
            swap(part).start()
        if part == 1:
            @pl.loop(1, 4)
            def _(d):
                gather_fx(d).start()
        if part == 2:
            second_of(0)
            second_of(1)
            send_relay(parts[0])
            send_plain(parts[0])
    second_of(2)
    second_of(3)
    send_relay(parts[1])
    send_plain(parts[1])
    rx[0, 4 + yi] = t3[rows(plane * WIDTH * 16, WIDTH * 16)]
    for j in range(1, CHUNKS):
        rx[j, 4 + yi] = t3[rows((j * 16 + plane) * WIDTH * 16, WIDTH * 16)]
    send_merged(parts[0])
    send_relay(parts[2])
    send_merged(parts[1])
    for j in range(1, CHUNKS):
        send_plain(parts[1 + j])
        if j == 1:
            wait(fxg.at[0:96], g_r)
            fxl[...] = stacked(fxg[...].T)
        if j + 1 < CHUNKS:
            send_relay(parts[2 + j])
        send_merged(parts[1 + j])
    for j in range(CHUNKS):
        if j == 0:
            await_part(0)
            await_part(1)
        else:
            await_part(j + 1)
        do_spread(j)
    for j in range(CHUNKS):
        wait(zr.at[j, 0:planes - 1], z_r.at[j])
        total(j)
    for a in range(4):
        out[a] = fin[pl.ds(a, 32, stride=4), :][:, :64]

    for n in range(4):
        swap(n).wait_send()
    wait(fxg.at[0:96], g_s)
    for n, part in enumerate(parts):
        for way in range(2):
            relay(part, way).wait_send()
        wait(dummy.at[0:11 * WIDTH * 16 // (2 if n < 2 else 1)], x_s.at[n])
    for j in range(CHUNKS):
        wait(zr.at[j, 0:planes - 1], z_s.at[j])


def body(zn, snapshot, factor_x, factor_y, factor_z):
    anywhere = pl.BlockSpec(memory_space=pl.ANY)
    dma = pltpu.SemaphoreType.DMA
    core = pl.pallas_call(
        functools.partial(kernel, zn),
        out_shape=pltpu.VMEM((4, 32, 64), F32),
        in_specs=[anywhere] * 4,
        out_specs=pl.BlockSpec(memory_space=pltpu.VMEM),
        scratch_shapes=[
            pltpu.VMEM((16, 2, 256, 128), F32),
            pltpu.VMEM((256, 128), F32),
            pltpu.VMEM((128, 128), F32),
            pltpu.VMEM((128, 128), F32),
            pltpu.VMEM((128, 256), F32),
            pltpu.VMEM((256, 256), BF16),
            pltpu.VMEM((256, 256), BF16),
            pltpu.VMEM((256, 256), BF16),
            pltpu.VMEM((16, 128, 128), F32),
            pltpu.VMEM((16, 128, 128), F32),
            pltpu.VMEM((16, 128, 128), F32),
            pltpu.VMEM((2048, 128), F32),
            pltpu.VMEM((CHUNKS, 12, WIDTH * 16, 128), F32),
            pltpu.VMEM((CHUNKS, 2, WIDTH * 32, 128), F32),
            pltpu.VMEM((CHUNKS, 4 * zn, 4 * PAIRS, 128), F32),
            pltpu.VMEM((CHUNKS, 4 * zn, 4 * PAIRS, 128), F32),
            pltpu.VMEM((128, 128), F32),
            dma((16,)), dma((3,)), dma((4,)), dma((4,)),
            dma((1 + CHUNKS, 2)), dma((1 + CHUNKS, 2)), dma((1 + CHUNKS,)), dma((1 + CHUNKS,)), dma((CHUNKS,)), dma((CHUNKS,)), dma, dma,
        ],
        compiler_params=pltpu.CompilerParams(
            collective_id=0, has_side_effects=True, vmem_limit_bytes=40 * 1024 * 1024
        ),
    )(*(pltpu.with_memory_space_constraint(a, pltpu.HBM) for a in (snapshot.reshape(2, 16, 256, 128), factor_x, factor_y, factor_z)))
    return core.transpose(0, 2, 1)


def solution(mesh):
    return jax.shard_map(
        functools.partial(body, mesh.shape["gx"] // 4),
        mesh=mesh,
        in_specs=(P("gx", "gy", "gz"), P("gx", None), P("gy", None), P("gz", None)),
        out_specs=P("gx", "gy", "gz"),
        check_vma=False,
    )
```

profile of v0, /device:TPU:6, one launch (start us, length us, event | category | flops | bytes accessed | tf_op | source)
XLA Modules:
  0.0 33.1 jit_solution(12735366379330330792)
XLA Ops:
  0.0 32.4 %shard_map.46 = f32[4,32,64]{2,1,0:T(8,128)S(1)} custom-call(f32[2,16,256,128]{3,2,1,0:T(8,128)} %bitcast.3, f32[32,128]{1,0:T(8,128)} %fx.1, f32[256,128]{1,0:T(8,128)} %fy.1, f32[128,128]{1,0:T(8,128)} %fz.1), custom_call_target="tpu_custom_call" | custom-call | tf_op jit(solution)/shard_map/pallas_call | solution.py:299
  32.4 0.6 %copy.6 = f32[4,64,32]{1,2,0:T(8,128)} copy(f32[4,64,32]{1,2,0:T(8,128)S(1)} %bitcast.2) | data formatting | bytes 65536
where the time goes:
time: 33.2 us; the launch traced here: 33.1 us
  Pallas kernels  32.4 us (98%)
  local copies, waits for them, and re-layouts  0.63 us (2%)
    pallas_call x1, Pallas kernels, body(): pl.pallas_call(functools.partial(kernel, zn), out_shape=pltpu.VMEM((4, 32...  32.4 us

commit v1 on v0

--- a/solution.py
+++ b/solution.py
@@ -33,7 +33,7 @@
 def kernel(
     zn, snap, fx, fy, fz, out,
     s_buf, fy_v, fz_v, fxg, ft, fyl, fzl, fxl, t1s, t1o, t1r, t3, rx, rx1, p, zr, fin,
-    s_sem, f_sem, ys, yr, r_s, r_r, x_s, x_r, z_s, z_r, g_s, g_r,
+    s_sem, f_sem, ys, yr, r_s, r_r, x_s, x_r, z_s, z_r, g_s, g_r, known,
 ):
     gx, core, xi = lax.axis_index("gx"), lax.axis_index("gy"), lax.axis_index("gz")
     zi, yi = gx // 4, lax.rem(gx, 4)
@@ -43,10 +43,6 @@
 
     right, opposite, left = lax.rem(xi + 1, 4), lax.rem(xi + 2, 4), lax.rem(xi + 3, 4)
 
-    def in_plane(d):
-        x, y = lax.rem(xi + d // 4, 4), lax.rem(yi + lax.rem(d, 4), 4)
-        return (zi * 4 + y, core, x)
-
     def in_column(d):
         z, y = lax.rem(zi + d // 4, zn), lax.rem(yi + lax.rem(d, 4), 4)
         return z * 4 + y, (z * 4 + y, core, xi)
@@ -59,44 +55,55 @@
     my_fx = fxg.at[rows(yi * 32, 32)]
     load_x = pltpu.make_async_copy(fx, my_fx, f_sem.at[2])
     load_y.start()
+    load_z.start()
+    load_x.start()
 
     @pl.loop(0, 16)
     def _(i):
         load(i).start()
 
-    load_z.start()
-    load_x.start()
 
     barrier = pltpu.get_barrier_semaphore()
     pl.semaphore_signal(barrier, inc=1, device_id=(gx, other, xi), device_id_type=MESH)
 
-    @pl.loop(1, 16)
+    for x in (left, right):
+        pl.semaphore_signal(barrier, inc=1, device_id=(gx, core, x), device_id_type=MESH)
+
+    @pl.loop(1, 4)
     def _(d):
-        pl.semaphore_signal(barrier, inc=1, device_id=in_plane(d), device_id_type=MESH)
-
-    @pl.loop(1, zn)
-    def _(d):
+        pl.semaphore_signal(barrier, inc=1, device_id=in_column(d)[1], device_id_type=MESH)
+
+    for d in (1, zn - 1):
         pl.semaphore_signal(barrier, inc=1, device_id=in_column(4 * d)[1], device_id_type=MESH)
+
+    def tell_x(stage):
+        for x in (left, right):
+            pl.semaphore_signal(known.at[stage], inc=1, device_id=(gx, core, x), device_id_type=MESH)
+
+    def tell_y(stage):
+        @pl.loop(1, 4)
+        def _(d):
+            pl.semaphore_signal(known.at[stage], inc=1, device_id=in_column(d)[1], device_id_type=MESH)
+
+    def tell_z(stage, distance):
+        for d in (distance, zn - distance):
+            pl.semaphore_signal(known.at[stage], inc=1, device_id=in_column(4 * d)[1], device_id_type=MESH)
 
     load_y.wait()
     ft[...] = fy_v[...].T
     high, low = split(jnp.concatenate([ft[rows(other * 64, 64)], ft[rows(core * 64, 64)]], axis=0))
     fyl[...] = jnp.concatenate([high, low], axis=0)
-    load_z.wait()
-    group = 4 * WIDTH
-    fz_t = fz_v[...].T
-    fzl[...] = stacked(jnp.concatenate(
-        [fz_t[32 * x + group * j:32 * x + group * (j + 1)] for j in range(CHUNKS) for x in range(4)], axis=0))
-
-    def first_of(i):
-        load(i).wait()
-        high, low = split(jnp.concatenate([s_buf[i, 0], s_buf[i, 1]], axis=1))
-        both = jnp.dot(fyl[...], high, preferred_element_type=F32)
-        t = both[:128] + both[128:] + jnp.dot(fyl[0:128], low, preferred_element_type=F32)
-        t1s[i, 0:64] = t[:64, :128]
-        t1s[i, 64:128] = t[:64, 128:]
-        t1o[i, 0:64] = t[64:, :128]
-        t1o[i, 64:128] = t[64:, 128:]
+    def first(part):
+        for i in range(4 * part, 4 * part + 4):
+            load(i).wait()
+        for i in range(4 * part, 4 * part + 4):
+            high, low = split(jnp.concatenate([s_buf[i, 0], s_buf[i, 1]], axis=1))
+            both = jnp.dot(fyl[...], high, preferred_element_type=F32)
+            t = both[:128] + both[128:] + jnp.dot(fyl[0:128], low, preferred_element_type=F32)
+            for h in range(2):
+                piece = t[:, 128 * h:128 * h + 128]
+                t1s[i, 64 * h:64 * h + 64] = piece[:64]
+                t1o[i, 64 * h:64 * h + 64] = piece[64:]
 
     def swap(part):
         at = pl.ds(4 * part, 4)
@@ -227,19 +234,21 @@
         size = slice(0, 11 * WIDTH * 16 // (2 if n < 2 else 1))
         wait(dummy.at[size], x_r.at[n])
 
-    def first(part):
-        @pl.loop(4 * part, 4 * part + 4)
-        def _(i):
-            first_of(i)
-
-    entered = lambda: pl.semaphore_wait(barrier, 1 + 15 + (zn - 1))
+    entered = lambda: pl.semaphore_wait(barrier, 8)
     for part in range(4):
         first(part)
         if part == 1:
+            load_z.wait()
+            group = 4 * WIDTH
+            fz_t = fz_v[...].T
+            fzl[...] = stacked(jnp.concatenate(
+                [fz_t[32 * x + group * j:32 * x + group * (j + 1)] for j in range(CHUNKS) for x in range(4)], axis=0))
             load_x.wait()
             entered()
             for n in range(part):
                 swap(n).start()
+            tell_x(0)
+            tell_z(1, 1)
         if part >= 1:
             swap(part).start()
         if part == 1:
@@ -250,17 +259,22 @@
             second_of(0)
             second_of(1)
             send_relay(parts[0])
+            pl.semaphore_wait(known.at[0], 2)
             send_plain(parts[0])
     second_of(2)
     second_of(3)
     send_relay(parts[1])
     send_plain(parts[1])
+    pl.semaphore_wait(known.at[1], 2)
+    tell_z(2, 2)
     rx[0, 4 + yi] = t3[rows(plane * WIDTH * 16, WIDTH * 16)]
     for j in range(1, CHUNKS):
         rx[j, 4 + yi] = t3[rows((j * 16 + plane) * WIDTH * 16, WIDTH * 16)]
     send_merged(parts[0])
     send_relay(parts[2])
     send_merged(parts[1])
+    pl.semaphore_wait(known.at[2], 2)
+    tell_y(3)
     for j in range(1, CHUNKS):
         send_plain(parts[1 + j])
         if j == 1:
@@ -269,6 +283,7 @@
         if j + 1 < CHUNKS:
             send_relay(parts[2 + j])
         send_merged(parts[1 + j])
+    pl.semaphore_wait(known.at[3], 3)
     for j in range(CHUNKS):
         if j == 0:
             await_part(0)
@@ -276,12 +291,6 @@
         else:
             await_part(j + 1)
         do_spread(j)
-    for j in range(CHUNKS):
-        wait(zr.at[j, 0:planes - 1], z_r.at[j])
-        total(j)
-    for a in range(4):
-        out[a] = fin[pl.ds(a, 32, stride=4), :][:, :64]
-
     for n in range(4):
         swap(n).wait_send()
     wait(fxg.at[0:96], g_s)
@@ -289,6 +298,12 @@
         for way in range(2):
             relay(part, way).wait_send()
         wait(dummy.at[0:11 * WIDTH * 16 // (2 if n < 2 else 1)], x_s.at[n])
+    for j in range(CHUNKS):
+        wait(zr.at[j, 0:planes - 1], z_r.at[j])
+        total(j)
+    for a in range(4):
+        out[a] = fin[pl.ds(a, 32, stride=4), :][:, :64]
+
     for j in range(CHUNKS):
         wait(zr.at[j, 0:planes - 1], z_s.at[j])
 
@@ -321,6 +336,7 @@
             pltpu.VMEM((128, 128), F32),
             dma((16,)), dma((3,)), dma((4,)), dma((4,)),
             dma((1 + CHUNKS, 2)), dma((1 + CHUNKS, 2)), dma((1 + CHUNKS,)), dma((1 + CHUNKS,)), dma((CHUNKS,)), dma((CHUNKS,)), dma, dma,
+            pltpu.SemaphoreType.REGULAR((4,)),
         ],
         compiler_params=pltpu.CompilerParams(
             collective_id=0, has_side_effects=True, vmem_limit_bytes=40 * 1024 * 1024

time: 33.2 us -> 31.1 us (0.937)
  Pallas kernels: 32.4 us -> 30.3 us
    pallas_call x1, Pallas kernels: 32.4 us -> 30.3 us  [body(): pl.pallas_call(functools.partial(kernel, zn), out_shape=pltpu.VMEM((4, 32...]
where the time goes in v1:
time: 31.1 us; the launch traced here: 31 us
  Pallas kernels  30.3 us (97%)
  local copies, waits for them, and re-layouts  0.63 us (2%)
    pallas_call x1, Pallas kernels, body(): pl.pallas_call(functools.partial(kernel, zn), out_shape=pltpu.VMEM((4, 32...  30.3 us
    unnamed x1, local copies, waits for them, and re-layouts  0.63 us

profile of v1, /device:TPU:6, one launch (start us, length us, event | category | flops | bytes accessed | tf_op | source)
XLA Modules:
  0.0 31.0 jit_solution(5161223315769849474)
XLA Ops:
  0.0 30.3 %shard_map.46 = f32[4,32,64]{2,1,0:T(8,128)S(1)} custom-call(f32[2,16,256,128]{3,2,1,0:T(8,128)} %bitcast.3, f32[32,128]{1,0:T(8,128)} %fx.1, f32[256,128]{1,0:T(8,128)} %fy.1, f32[128,128]{1,0:T(8,128)} %fz.1), custom_call_target="tpu_custom_call" | custom-call | tf_op jit(solution)/shard_map/pallas_call | solution.py:314
  30.3 0.6 %copy.6 = f32[4,64,32]{1,2,0:T(8,128)} copy(f32[4,64,32]{1,2,0:T(8,128)S(1)} %bitcast.2) | data formatting | bytes 65536

commit v2 on v1

--- a/solution.py
+++ b/solution.py
@@ -61,7 +61,6 @@
     @pl.loop(0, 16)
     def _(i):
         load(i).start()
-
 
     barrier = pltpu.get_barrier_semaphore()
     pl.semaphore_signal(barrier, inc=1, device_id=(gx, other, xi), device_id_type=MESH)
@@ -127,7 +126,7 @@
         at = ((j * 4 + x) * 4 + y) * WIDTH
         if h is None:
             return t3.at[pl.ds(pl.multiple_of(at * 16, 32), number * 16)]
-        return t3.reshape(128, 2, 8, 128).at[pl.ds(at, number), h]
+        return t3.reshape(129, 2, 8, 128).at[pl.ds(at, number), h]
 
     def slot_of(ref, part, at):
         j, h = part[:2]
@@ -237,7 +236,7 @@
     entered = lambda: pl.semaphore_wait(barrier, 8)
     for part in range(4):
         first(part)
-        if part == 1:
+        if part == 0:
             load_z.wait()
             group = 4 * WIDTH
             fz_t = fz_v[...].T
@@ -249,8 +248,7 @@
                 swap(n).start()
             tell_x(0)
             tell_z(1, 1)
-        if part >= 1:
-            swap(part).start()
+        swap(part).start()
         if part == 1:
             @pl.loop(1, 4)
             def _(d):
@@ -328,12 +326,12 @@
             pltpu.VMEM((16, 128, 128), F32),
             pltpu.VMEM((16, 128, 128), F32),
             pltpu.VMEM((16, 128, 128), F32),
-            pltpu.VMEM((2048, 128), F32),
+            pltpu.VMEM((2064, 128), F32),
             pltpu.VMEM((CHUNKS, 12, WIDTH * 16, 128), F32),
             pltpu.VMEM((CHUNKS, 2, WIDTH * 32, 128), F32),
             pltpu.VMEM((CHUNKS, 4 * zn, 4 * PAIRS, 128), F32),
             pltpu.VMEM((CHUNKS, 4 * zn, 4 * PAIRS, 128), F32),
-            pltpu.VMEM((128, 128), F32),
+            pltpu.VMEM((136, 128), F32),
             dma((16,)), dma((3,)), dma((4,)), dma((4,)),
             dma((1 + CHUNKS, 2)), dma((1 + CHUNKS, 2)), dma((1 + CHUNKS,)), dma((1 + CHUNKS,)), dma((CHUNKS,)), dma((CHUNKS,)), dma, dma,
             pltpu.SemaphoreType.REGULAR((4,)),

time: 31.1 us -> 31.1 us (level)
  no operation moved by 1% of the time
where the time goes in v2:
time: 31.1 us; the launch traced here: 31 us
  Pallas kernels  30.4 us (98%)
  local copies, waits for them, and re-layouts  0.63 us (2%)
    pallas_call x1, Pallas kernels, body(): pl.pallas_call(functools.partial(kernel, zn), out_shape=pltpu.VMEM((4, 32...  30.4 us
    unnamed x1, local copies, waits for them, and re-layouts  0.63 us

profile of v2, /device:TPU:6, one launch (start us, length us, event | category | flops | bytes accessed | tf_op | source)
XLA Modules:
  0.0 31.0 jit_solution(12721795874844348923)
XLA Ops:
  0.0 30.4 %shard_map.46 = f32[4,32,64]{2,1,0:T(8,128)S(1)} custom-call(f32[2,16,256,128]{3,2,1,0:T(8,128)} %bitcast.3, f32[32,128]{1,0:T(8,128)} %fx.1, f32[256,128]{1,0:T(8,128)} %fy.1, f32[128,128]{1,0:T(8,128)} %fz.1), custom_call_target="tpu_custom_call" | custom-call | tf_op jit(solution)/shard_map/pallas_call | solution.py:312
  30.4 0.6 %copy.6 = f32[4,64,32]{1,2,0:T(8,128)} copy(f32[4,64,32]{1,2,0:T(8,128)S(1)} %bitcast.2) | data formatting | bytes 65536

commit v3 on v2

--- a/solution.py
+++ b/solution.py
@@ -91,14 +91,13 @@
     load_y.wait()
     ft[...] = fy_v[...].T
     high, low = split(jnp.concatenate([ft[rows(other * 64, 64)], ft[rows(core * 64, 64)]], axis=0))
-    fyl[...] = jnp.concatenate([high, low], axis=0)
+    fyl[...] = jnp.concatenate([high, low, high], axis=1)
     def first(part):
         for i in range(4 * part, 4 * part + 4):
             load(i).wait()
         for i in range(4 * part, 4 * part + 4):
             high, low = split(jnp.concatenate([s_buf[i, 0], s_buf[i, 1]], axis=1))
-            both = jnp.dot(fyl[...], high, preferred_element_type=F32)
-            t = both[:128] + both[128:] + jnp.dot(fyl[0:128], low, preferred_element_type=F32)
+            t = jnp.dot(fyl[...], jnp.concatenate([high, high, low], axis=0), preferred_element_type=F32)
             for h in range(2):
                 piece = t[:, 128 * h:128 * h + 128]
                 t1s[i, 64 * h:64 * h + 64] = piece[:64]
@@ -253,7 +252,7 @@
             @pl.loop(1, 4)
             def _(d):
                 gather_fx(d).start()
-        if part == 2:
+        if part == 3:
             second_of(0)
             second_of(1)
             send_relay(parts[0])
@@ -320,7 +319,7 @@
             pltpu.VMEM((128, 128), F32),
             pltpu.VMEM((128, 128), F32),
             pltpu.VMEM((128, 256), F32),
-            pltpu.VMEM((256, 256), BF16),
+            pltpu.VMEM((128, 768), BF16),
             pltpu.VMEM((256, 256), BF16),
             pltpu.VMEM((256, 256), BF16),
             pltpu.VMEM((16, 128, 128), F32),

time: 31.1 us -> 30.8 us (level)
  Pallas kernels: 30.4 us -> 30 us
    pallas_call x1, Pallas kernels: 30.4 us -> 30 us  [body(): pl.pallas_call(functools.partial(kernel, zn), out_shape=pltpu.VMEM((4, 32...]
where the time goes in v3:
time: 30.8 us; the launch traced here: 30.7 us
  Pallas kernels  30 us (97%)
  local copies, waits for them, and re-layouts  0.63 us (2%)
    pallas_call x1, Pallas kernels, body(): pl.pallas_call(functools.partial(kernel, zn), out_shape=pltpu.VMEM((4, 32...  30 us
    unnamed x1, local copies, waits for them, and re-layouts  0.63 us

profile of v3, /device:TPU:6, one launch (start us, length us, event | category | flops | bytes accessed | tf_op | source)
XLA Modules:
  0.0 30.7 jit_solution(17783389500175978811)
XLA Ops:
  0.0 30.0 %shard_map.46 = f32[4,32,64]{2,1,0:T(8,128)S(1)} custom-call(f32[2,16,256,128]{3,2,1,0:T(8,128)} %bitcast.3, f32[32,128]{1,0:T(8,128)} %fx.1, f32[256,128]{1,0:T(8,128)} %fy.1, f32[128,128]{1,0:T(8,128)} %fz.1), custom_call_target="tpu_custom_call" | custom-call | tf_op jit(solution)/shard_map/pallas_call | solution.py:311
  30.1 0.6 %copy.6 = f32[4,64,32]{1,2,0:T(8,128)} copy(f32[4,64,32]{1,2,0:T(8,128)S(1)} %bitcast.2) | data formatting | bytes 65536

commit v4 on v3

--- a/solution.py
+++ b/solution.py
@@ -150,14 +150,14 @@
             device_id=(zi * 4 + y, core, x), device_id_type=MESH).start()
 
     def send_plain(part):
-        @pl.loop(1, 4)
-        def _(d):
-            exchange(part, xi, lax.rem(yi + d, 4), 1)
-
         @pl.loop(0, 2)
         def _(y):
             exchange(part, right, y + 2, 0)
             exchange(part, left, y, 2)
+
+        @pl.loop(1, 4)
+        def _(d):
+            exchange(part, xi, lax.rem(yi + d, 4), 1)
 
     def send_merged(part):
         for way in range(2):

time: 30.8 us -> 30.8 us (level)
  no operation moved by 1% of the time
where the time goes in v4:
time: 30.8 us; the launch traced here: 30.7 us
  Pallas kernels  30 us (97%)
  local copies, waits for them, and re-layouts  0.63 us (2%)
    pallas_call x1, Pallas kernels, body(): pl.pallas_call(functools.partial(kernel, zn), out_shape=pltpu.VMEM((4, 32...  30 us
    unnamed x1, local copies, waits for them, and re-layouts  0.63 us

profile of v4, /device:TPU:6, one launch (start us, length us, event | category | flops | bytes accessed | tf_op | source)
XLA Modules:
  0.0 30.7 jit_solution(7494599947045618469)
XLA Ops:
  0.0 30.0 %shard_map.46 = f32[4,32,64]{2,1,0:T(8,128)S(1)} custom-call(f32[2,16,256,128]{3,2,1,0:T(8,128)} %bitcast.3, f32[32,128]{1,0:T(8,128)} %fx.1, f32[256,128]{1,0:T(8,128)} %fy.1, f32[128,128]{1,0:T(8,128)} %fz.1), custom_call_target="tpu_custom_call" | custom-call | tf_op jit(solution)/shard_map/pallas_call | solution.py:311
  30.0 0.6 %copy.6 = f32[4,64,32]{1,2,0:T(8,128)} copy(f32[4,64,32]{1,2,0:T(8,128)S(1)} %bitcast.2) | data formatting | bytes 65536
